TPU v7x, 32 devices: a whole 2x2x4 slice. The times are simulated.
32 devices in a mesh: groups: 2 (over x), chan: 16 (over z, y, core).
Axes of the slice: x: 2, y: 2, z: 4, core: 2. Of those that a mesh axis runs over, the one named last changes fastest.
Arguments:
- raw: bfloat16 [5120, 4096], P('chan', 'groups'), parts along dimension 1, may hold values from -50 to 50
- taps: bfloat16 [255], replicated, may hold values from -0.375 to 0.375
- tile_dist: int32 [16, 8], P('chan', 'groups'), parts along dimension 1, may hold values from 1 to 4, as said below
- tile_count: int32 [32], P(('groups', 'chan')), parts along dimension 0, may hold values from 0 to 4
- owner: int32 [8], P('groups'), parts along dimension 0, may hold values from 0 to 15, as said below
Outputs:
- band_stack: float32 [16, 256, 128], P('chan', 'groups'), parts along dimension 1
There are 2 independent parts, one for each index of `groups`. A program takes and returns all parts, laid end to end along the dimension named above; an argument that names none is the same for every part. Nothing has to cross between parts.
Inputs may be any that keep to these rules, and one draw needn't show every extreme that they name: Each row of tile_dist holds every distance of 1 to 4 once; in row i the first tile_count[i] entries d satisfy i + d < 16. `owner`: the owners are distinct, and some band is owned by index 15.
All inputs are finite; a program needn't handle non-finite values.
Results may differ from a plain program's by a relative error of at most 0.014.
Values may be sent and summed in bfloat16 or wider, within the bound.
A program may use at most 128 MiB of HBM per device.

v0:
```python
import math
import jax
import jax.numpy as jnp
from jax import lax
from jax.sharding import PartitionSpec as P


def extended(x, sides, width):
    for axis, dim in sides:
        size, length = (lax.axis_size(axis), x.shape[dim])
        up = [(i, (i + 1) % size) for i in range(size - 1)]
        down = [(j, i) for i, j in up]
        last = lax.slice_in_dim(x, length - width, length, axis=dim)
        initial = lax.slice_in_dim(x, 0, width, axis=dim)
        before = lax.ppermute(last, axis, up)
        after = lax.ppermute(initial, axis, down)
        x = jnp.concatenate([before, x, after], axis=dim)
    return x


def passed_along(x, axis, by):
    size = lax.axis_size(axis)
    pairs = [(i, i + by) for i in range(size) if 0 <= i + by < size]
    return lax.ppermute(x, axis, pairs)


def band_matrix(taps, out_rows, in_cols):
    width = taps.shape[0]
    offset = (
        jnp.arange(in_cols, dtype=jnp.int32)[None, :]
        - 5 * jnp.arange(out_rows, dtype=jnp.int32)[:, None]
    )
    inside = (offset >= 0) & (offset < width)
    picked = jnp.take(taps, jnp.clip(offset, 0, width - 1))
    return jnp.where(inside, picked, jnp.zeros_like(picked))


def whiten(block):
    length, channels = block.shape
    bins = length // 16
    freqs = jnp.arange(1, bins + 1, dtype=jnp.int32)[:, None]
    times = jnp.arange(length, dtype=jnp.int32)[None, :]
    angle = (freqs * times % length).astype(jnp.float32) * (2.0 * math.pi / length)
    table = jnp.concatenate([jnp.cos(angle), -jnp.sin(angle)], axis=0)
    table_high = table.astype(jnp.bfloat16)
    table_low = (table - table_high.astype(jnp.float32)).astype(jnp.bfloat16)
    spectrum = jnp.dot(table_high, block, preferred_element_type=jnp.float32)
    spectrum = spectrum + jnp.dot(table_low, block, preferred_element_type=jnp.float32)
    squares = spectrum * spectrum
    power = jnp.sum(squares[:bins] + squares[bins:], axis=1) / (2 * channels)
    gain = lax.rsqrt(power + 1e-06)
    return (spectrum * jnp.concatenate([gain, gain])[:, None]).astype(jnp.bfloat16)


def cross_tile(mine, partner, scale):
    product = lax.dot_general(
        mine, partner, (((0,), (0,)), ((), ())), preferred_element_type=jnp.float32
    )
    return product * scale


def shards(raw, taps, tile_dist, tile_count, owner):
    rows = raw.shape[0]
    width = taps.shape[0]
    half = (width - 1) // 2
    out_rows = rows // 5
    banded = band_matrix(taps, out_rows, rows + 2 * half)
    padded = extended(raw, (("chan", 0),), half)
    filtered = jnp.dot(banded, padded, preferred_element_type=jnp.float32)
    decimated = filtered.astype(jnp.bfloat16)
    regrouped = lax.all_to_all(decimated, "chan", split_axis=1, concat_axis=0, tiled=True)
    whitened = whiten(regrouped)
    channels = whitened.shape[1]
    scale = 1.0 / whitened.shape[0]
    bands = tile_dist.shape[1]
    slots = jnp.arange(bands, dtype=jnp.int32) < tile_count[0]
    partner = whitened
    stacks = []
    for distance in range(1, bands + 1):
        partner = passed_along(whitened, "chan", -distance)
        listed = jnp.sum(((tile_dist[0] == distance) & slots).astype(jnp.int32))
        tile = lax.cond(
            listed > 0,
            lambda first, second: cross_tile(first, second, scale),
            lambda first, second: jnp.zeros((channels, channels), jnp.float32),
            whitened,
            partner,
        )
        stacks.append(tile)
    stacked = jnp.stack(stacks)
    totals = lax.psum(stacked, "chan")
    selected = (owner == lax.axis_index("chan")).astype(jnp.float32)
    return jnp.einsum("b,bxy->xy", selected, totals, precision=lax.Precision.HIGHEST)[None]


def solution(mesh):
    in_specs = (P("chan", "groups"), P(), P("chan", "groups"), P(("groups", "chan")), P("groups"))
    out_specs = P("chan", "groups", None)
    return jax.shard_map(shards, mesh=mesh, in_specs=in_specs, out_specs=out_specs, check_vma=False)
```

profile of v0, /device:TPU:1, one launch (start us, length us, event | category | flops | bytes accessed | tf_op | source)
XLA Modules:
  0.0 350.2 jit_solution(16321516343890510298)
XLA Ops:
  6.5 1.3 fusion.63
  7.9 4.5 %collective-permute-start = (bf16[127,2048]{1,0:T(8,128)(2,1)S(1)}, bf16[127,2048]{1,0:T(8,128)(2,1)S(1)}, u32[]{:S(2)}, u32[]{:S(2)}) collective-permute-start(bf16[127,2048]{1,0:T(8,128)(2,1)S(1)} %get-tuple-element.49), channel_id=1, source_target_pairs={{0,1},{1,2},{2,3},{3,4},{4,5},{5,6},{6,7},{7,8},{8,9},{9,10},{10,1... | collective-permute-start | bytes 1560584 | tf_op jit(solution)/shard_map/ppermute | solution.py:15
  12.4 1.9 collective-permute-start.1
  14.4 0.1 compare_select_fusion
  14.5 0.2 reshape.83
  14.7 202.9 %gather_fusion = bf16[36736]{0:T(1024)(128)(2,1)S(1)} fusion(bf16[255]{0:T(256)(128)(2,1)S(1)} %copy-done, s32[36864]{0:T(1024)S(1)} %pad_clamp_fusion), kind=kCustom, calls=%fused_computation | custom fusion | bytes 293888 | tf_op jit(solution)/shard_map/jit(_take)/gather | solution.py:34
  217.7 0.2 reshape.82
  217.9 1.9 fusion.13
  219.8 0.8 copy.13
  220.6 6.5 %all-to-all-start = ((bf16[64,16,128]{2,0,1:T(8,128)(2,1)}), bf16[64,16,128]{2,0,1:T(8,128)(2,1)S(1)}, u32[]{:S(2)}, u32[]{:S(2)}) async-start(bf16[64,16,128]{2,0,1:T(8,128)(2,1)} %bitcast.58), calls=%async_computation | async-start | bytes 524288 | tf_op jit(solution)/shard_map/all_to_all | solution.py:71
  227.1 0.0 all-reduce.2.cloned.1.call-start
  227.8 1.1 fusion.35
  228.9 7.7 %all-to-all-done = bf16[64,16,128]{2,0,1:T(8,128)(2,1)S(1)} async-done(((bf16[64,16,128]{2,0,1:T(8,128)(2,1)}), bf16[64,16,128]{2,0,1:T(8,128)(2,1)S(1)}, u32[]{:S(2)}, u32[]{:S(2)}) %all-to-all-start) | async-done | bytes 262176 | tf_op jit(solution)/shard_map/all_to_all | solution.py:71
  236.5 0.2 fusion.17
  236.8 0.2 fusion.64
  237.0 0.1 fusion.43
  237.1 0.1 pad_maximum_fusion.2
  237.2 0.1 multiply_convert_fusion
  237.3 2.6 collective-permute-start.2
  239.9 1.3 collective-permute-start.3
  241.2 1.3 collective-permute-start.4
  242.5 1.3 collective-permute-start.5
  243.8 0.7 fusion.50
  247.1 0.2 conditional.5
  247.1 0.2 fusion.1
  247.3 0.5 collective-permute-done.4
  247.8 1.3 collective-permute-done.5
  249.2 0.2 conditional.7
  249.2 0.2 fusion.3
  249.4 0.7 pad_maximum_fusion.1
  250.1 91.1 %all-reduce.2.cloned.1.call-done = f32[4,128,128]{2,1,0:T(8,128)} async-done(((f32[4,128,128]{2,1,0:T(8,128)}), f32[4,128,128]{2,1,0:T(8,128)}) %all-reduce.2.cloned.1.call-update) | async-done | bytes 262160 | tf_op jit(solution)/shard_map/psum | solution.py:91
  341.3 2.1 fusion.22
  (21 shorter events, 0.1 us)
Async XLA Ops:
  6.5 8.2 %copy-start = (bf16[255]{0:T(256)(128)(2,1)S(1)}, bf16[255]{0:T(256)(128)(2,1)}, u32[]{:S(2)}) copy-start(bf16[255]{0:T(256)(128)(2,1)} %param.14) | copy-start | bytes 1534
  7.9 210.0 %collective-permute-start = (bf16[127,2048]{1,0:T(8,128)(2,1)S(1)}, bf16[127,2048]{1,0:T(8,128)(2,1)S(1)}, u32[]{:S(2)}, u32[]{:S(2)}) collective-permute-start(bf16[127,2048]{1,0:T(8,128)(2,1)S(1)} %get-tuple-element.49), channel_id=1, source_target_pairs={{0,1},{1,2},{2,3},{3,4},{4,5},{5,6},{6,7},{7,8},{8,9},{9,10},{10,1... | collective-permute-start | bytes 1560584 | tf_op jit(solution)/shard_map/ppermute | solution.py:15
  12.4 205.5 %collective-permute-start.1 = (bf16[127,2048]{1,0:T(8,128)(2,1)S(1)}, bf16[127,2048]{1,0:T(8,128)(2,1)}, u32[]{:S(2)}, u32[]{:S(2)}) collective-permute-start(bf16[127,2048]{1,0:T(8,128)(2,1)S(1)} %get-tuple-element.50), channel_id=1, source_target_pairs={{1,0},{2,1},{3,2},{4,3},{5,4},{6,5},{7,6},{8,7},{9,8},{10,9},{11,1... | collective-permute-start | bytes 1560584 | tf_op jit(solution)/shard_map/ppermute | solution.py:16
  14.7 203.2 %copy-start.1 = (bf16[320,2048]{1,0:T(8,128)(2,1)S(1)}, bf16[320,2048]{1,0:T(8,128)(2,1)}, u32[]{:S(2)}) copy-start(bf16[320,2048]{1,0:T(8,128)(2,1)} %param.13) | copy-start | bytes 3932164
  220.6 15.9 %all-to-all-start = ((bf16[64,16,128]{2,0,1:T(8,128)(2,1)}), bf16[64,16,128]{2,0,1:T(8,128)(2,1)S(1)}, u32[]{:S(2)}, u32[]{:S(2)}) async-start(bf16[64,16,128]{2,0,1:T(8,128)(2,1)} %bitcast.58), calls=%async_computation | async-start | bytes 524288 | tf_op jit(solution)/shard_map/all_to_all | solution.py:71
  227.0 16.7 %copy-start.3 = (s32[1,4]{1,0:T(1,128)S(1)}, s32[1,4]{1,0:T(1,128)}, u32[]{:S(2)}) copy-start(s32[1,4]{1,0:T(1,128)} %param.15) | copy-start | bytes 52
  227.1 114.2 %all-reduce.2.cloned.1.call-start = ((), (), s32[]{:S(2)}) async-start(), calls=%async_computation.1 | async-start | bytes 524288 | tf_op jit(solution)/shard_map/psum | solution.py:91
  236.8 104.5 %copy-start.2 = (s32[4]{0:T(128)S(1)}, s32[4]{0:T(128)}, u32[]{:S(2)}) copy-start(s32[4]{0:T(128)} %param.17) | copy-start | bytes 52
  237.3 9.7 %collective-permute-start.2 = (bf16[128,128]{1,0:T(8,128)(2,1)S(1)}, bf16[128,128]{1,0:T(8,128)(2,1)S(1)}, u32[]{:S(2)}, u32[]{:S(2)}) collective-permute-start(bf16[128,128]{1,0:T(8,128)(2,1)S(1)} %multiply_convert_fusion), channel_id=1, source_target_pairs={{1,0},{2,1},{3,2},{4,3},{5,4},{6,5},{7,6},{8,7},{9,8},{10,9},{11,1... | collective-permute-start | bytes 98312 | tf_op jit(solution)/shard_map/ppermute | solution.py:24
  239.9 7.2 %collective-permute-start.3 = (bf16[128,128]{1,0:T(8,128)(2,1)S(1)}, bf16[128,128]{1,0:T(8,128)(2,1)S(1)}, u32[]{:S(2)}, u32[]{:S(2)}) collective-permute-start(bf16[128,128]{1,0:T(8,128)(2,1)S(1)} %multiply_convert_fusion), channel_id=1, source_target_pairs={{2,0},{3,1},{4,2},{5,3},{6,4},{7,5},{8,6},{9,7},{10,8},{11,9},{12,... | collective-permute-start | bytes 98312 | tf_op jit(solution)/shard_map/ppermute | solution.py:24
  241.2 6.7 %collective-permute-start.4 = (bf16[128,128]{1,0:T(8,128)(2,1)S(1)}, bf16[128,128]{1,0:T(8,128)(2,1)S(1)}, u32[]{:S(2)}, u32[]{:S(2)}) collective-permute-start(bf16[128,128]{1,0:T(8,128)(2,1)S(1)} %multiply_convert_fusion), channel_id=1, source_target_pairs={{3,0},{4,1},{5,2},{6,3},{7,4},{8,5},{9,6},{10,7},{11,8},{12,9},{13... | collective-permute-start | bytes 98312 | tf_op jit(solution)/shard_map/ppermute | solution.py:24
  242.5 6.7 %collective-permute-start.5 = (bf16[128,128]{1,0:T(8,128)(2,1)S(1)}, bf16[128,128]{1,0:T(8,128)(2,1)S(1)}, u32[]{:S(2)}, u32[]{:S(2)}) collective-permute-start(bf16[128,128]{1,0:T(8,128)(2,1)S(1)} %multiply_convert_fusion), channel_id=1, source_target_pairs={{4,0},{5,1},{6,2},{7,3},{8,4},{9,5},{10,6},{11,7},{12,8},{13,9},{1... | collective-permute-start | bytes 98312 | tf_op jit(solution)/shard_map/ppermute | solution.py:24
Sparse Core Ops, SparseCore 0:
  250.2 90.9 all-reduce.1
where the time goes:
time: 351 us; the launch traced here: 350 us
  local copies, waits for them, and re-layouts  205 us (58%)
  waiting for transfers between devices  101 us (29%)
  starting transfers between devices  19.4 us (6%)
  between operations  16.8 us (5%)
  matrix products  4.78 us (1%)
    gather x2, local copies, waits for them, and re-layouts, band_matrix(): picked = jnp.take(taps, jnp.clip(offset, 0, width - 1))  203 us
    psum x1, waiting for transfers between devices, shards(): totals = lax.psum(stacked, 'chan')  91.1 us
    all_to_all x1, waiting for transfers between devices, shards(): lax.all_to_all(decimated, 'chan', split_axis=1, concat_axis=0, tiled=True)  7.67 us
  transfers between devices with their start and end apart: 8, of which 4 were waited for; matrix products, arithmetic and copies ran while one was open for 59% of the time, Pallas kernels for 0%

commit v1 on v0

--- a/solution.py
+++ b/solution.py
@@ -88,7 +88,8 @@
         )
         stacks.append(tile)
     stacked = jnp.stack(stacks)
-    totals = lax.psum(stacked, "chan")
+    blocks = lax.all_gather(stacked, "chan")
+    totals = jnp.sum(blocks, axis=0)
     selected = (owner == lax.axis_index("chan")).astype(jnp.float32)
     return jnp.einsum("b,bxy->xy", selected, totals, precision=lax.Precision.HIGHEST)[None]
 

time: 351 us -> 314 us (0.89)
  waiting for transfers between devices: 101 us -> 62.2 us
    psum x1 -> x0, waiting for transfers between devices: 91.1 us -> none  [shards(): totals = lax.psum(stacked, 'chan')]
    all_gather x0 -> x1, waiting for transfers between devices: none -> 52.6 us  [shards(): blocks = lax.all_gather(stacked, 'chan')]
  transfers between devices with their start and end apart: 8 -> 8, of which waited for: 4 -> 4; matrix products, arithmetic and copies ran while one was open for 59% -> 66% of each run, Pallas kernels for 0% -> 0%
where the time goes in v1:
time: 314 us; the launch traced here: 313 us
  local copies, waits for them, and re-layouts  205 us (65%)
  waiting for transfers between devices  62.2 us (20%)
  starting transfers between devices  19.4 us (6%)
  between operations  16.8 us (5%)
  other arithmetic  5.39 us (2%)
  matrix products  3.83 us (1%)
    gather x2, local copies, waits for them, and re-layouts, band_matrix(): picked = jnp.take(taps, jnp.clip(offset, 0, width - 1))  203 us
    all_gather x1, waiting for transfers between devices, shards(): blocks = lax.all_gather(stacked, 'chan')  52.6 us
    all_to_all x1, waiting for transfers between devices, shards(): lax.all_to_all(decimated, 'chan', split_axis=1, concat_axis=0, tiled=True)  7.68 us
    all_to_all x1, starting transfers between devices, shards(): lax.all_to_all(decimated, 'chan', split_axis=1, concat_axis=0, tiled=True)  6.45 us
    ppermute x4, starting transfers between devices, passed_along(): return lax.ppermute(x, axis, pairs)  6.44 us
  transfers between devices with their start and end apart: 8, of which 4 were waited for; matrix products, arithmetic and copies ran while one was open for 66% of the time, Pallas kernels for 0%

profile of v1, /device:TPU:1, one launch (start us, length us, event | category | flops | bytes accessed | tf_op | source)
XLA Modules:
  0.0 313.2 jit_solution(1108697610887840078)
XLA Ops:
  6.5 1.4 fusion.63
  7.9 4.5 %collective-permute-start = (bf16[127,2048]{1,0:T(8,128)(2,1)S(1)}, bf16[127,2048]{1,0:T(8,128)(2,1)S(1)}, u32[]{:S(2)}, u32[]{:S(2)}) collective-permute-start(bf16[127,2048]{1,0:T(8,128)(2,1)S(1)} %get-tuple-element.49), channel_id=1, source_target_pairs={{0,1},{1,2},{2,3},{3,4},{4,5},{5,6},{6,7},{7,8},{8,9},{9,10},{10,1... | collective-permute-start | bytes 1560584 | tf_op jit(solution)/shard_map/ppermute | solution.py:15
  12.5 1.9 collective-permute-start.1
  14.4 0.1 compare_select_fusion
  14.5 0.2 reshape.83
  14.8 202.9 %gather_fusion = bf16[36736]{0:T(1024)(128)(2,1)S(1)} fusion(bf16[255]{0:T(256)(128)(2,1)S(1)} %copy-done, s32[36864]{0:T(1024)S(1)} %pad_clamp_fusion), kind=kCustom, calls=%fused_computation | custom fusion | bytes 293888 | tf_op jit(solution)/shard_map/jit(_take)/gather | solution.py:34
  217.7 0.2 reshape.82
  218.0 1.9 fusion.13
  219.9 0.8 copy.14
  220.6 6.5 %all-to-all-start = ((bf16[64,16,128]{2,0,1:T(8,128)(2,1)}), bf16[64,16,128]{2,0,1:T(8,128)(2,1)S(1)}, u32[]{:S(2)}, u32[]{:S(2)}) async-start(bf16[64,16,128]{2,0,1:T(8,128)(2,1)} %bitcast.59), calls=%async_computation | async-start | bytes 524288 | tf_op jit(solution)/shard_map/all_to_all | solution.py:71
  227.8 1.1 fusion.35
  228.9 7.7 %all-to-all-done = bf16[64,16,128]{2,0,1:T(8,128)(2,1)S(1)} async-done(((bf16[64,16,128]{2,0,1:T(8,128)(2,1)}), bf16[64,16,128]{2,0,1:T(8,128)(2,1)S(1)}, u32[]{:S(2)}, u32[]{:S(2)}) %all-to-all-start) | async-done | bytes 262176 | tf_op jit(solution)/shard_map/all_to_all | solution.py:71
  236.6 0.2 fusion.17
  236.8 0.2 fusion.64
  237.0 0.1 fusion.43
  237.1 0.1 pad_maximum_fusion.2
  237.2 0.1 multiply_convert_fusion
  237.3 2.6 collective-permute-start.2
  239.9 1.3 collective-permute-start.3
  241.2 1.3 collective-permute-start.4
  242.5 1.3 collective-permute-start.5
  243.8 0.7 fusion.50
  247.1 0.2 conditional.5
  247.1 0.2 fusion.1
  247.3 0.6 collective-permute-done.4
  247.9 1.3 collective-permute-done.5
  249.2 0.2 conditional.7
  249.2 0.2 fusion.3
  249.4 0.7 pad_maximum_fusion.1
  250.2 52.6 %all-gather.3.cloned.1.call-done = f32[64,128,128]{2,1,0:T(8,128)} async-done(((f32[4,128,128]{2,1,0:T(8,128)}), f32[64,128,128]{2,1,0:T(8,128)}) %all-gather.3.cloned.1.call-update) | async-done | bytes 4194320 | tf_op jit(solution)/shard_map/all_gather | solution.py:91
  302.8 2.4 reduce_sum.59
  305.2 1.1 fusion.22
  (22 shorter events, 0.2 us)
Async XLA Ops:
  6.5 8.2 %copy-start = (bf16[255]{0:T(256)(128)(2,1)S(1)}, bf16[255]{0:T(256)(128)(2,1)}, u32[]{:S(2)}) copy-start(bf16[255]{0:T(256)(128)(2,1)} %param.14) | copy-start | bytes 1534
  7.9 210.0 %collective-permute-start = (bf16[127,2048]{1,0:T(8,128)(2,1)S(1)}, bf16[127,2048]{1,0:T(8,128)(2,1)S(1)}, u32[]{:S(2)}, u32[]{:S(2)}) collective-permute-start(bf16[127,2048]{1,0:T(8,128)(2,1)S(1)} %get-tuple-element.49), channel_id=1, source_target_pairs={{0,1},{1,2},{2,3},{3,4},{4,5},{5,6},{6,7},{7,8},{8,9},{9,10},{10,1... | collective-permute-start | bytes 1560584 | tf_op jit(solution)/shard_map/ppermute | solution.py:15
  12.5 205.5 %collective-permute-start.1 = (bf16[127,2048]{1,0:T(8,128)(2,1)S(1)}, bf16[127,2048]{1,0:T(8,128)(2,1)}, u32[]{:S(2)}, u32[]{:S(2)}) collective-permute-start(bf16[127,2048]{1,0:T(8,128)(2,1)S(1)} %get-tuple-element.50), channel_id=1, source_target_pairs={{1,0},{2,1},{3,2},{4,3},{5,4},{6,5},{7,6},{8,7},{9,8},{10,9},{11,1... | collective-permute-start | bytes 1560584 | tf_op jit(solution)/shard_map/ppermute | solution.py:16
  14.8 203.2 %copy-start.1 = (bf16[320,2048]{1,0:T(8,128)(2,1)S(1)}, bf16[320,2048]{1,0:T(8,128)(2,1)}, u32[]{:S(2)}) copy-start(bf16[320,2048]{1,0:T(8,128)(2,1)} %param.13) | copy-start | bytes 3932164
  219.8 23.9 %copy-start.3 = (s32[1,4]{1,0:T(1,128)S(1)}, s32[1,4]{1,0:T(1,128)}, u32[]{:S(2)}) copy-start(s32[1,4]{1,0:T(1,128)} %param.15) | copy-start | bytes 52
  220.6 15.9 %all-to-all-start = ((bf16[64,16,128]{2,0,1:T(8,128)(2,1)}), bf16[64,16,128]{2,0,1:T(8,128)(2,1)S(1)}, u32[]{:S(2)}, u32[]{:S(2)}) async-start(bf16[64,16,128]{2,0,1:T(8,128)(2,1)} %bitcast.59), calls=%async_computation | async-start | bytes 524288 | tf_op jit(solution)/shard_map/all_to_all | solution.py:71
  227.1 75.7 %all-gather.3.cloned.1.call-start = ((), (), s32[]{:S(2)}) async-start(), calls=%async_computation.1 | async-start | bytes 4456448 | tf_op jit(solution)/shard_map/all_gather | solution.py:91
  237.3 9.7 %collective-permute-start.2 = (bf16[128,128]{1,0:T(8,128)(2,1)S(1)}, bf16[128,128]{1,0:T(8,128)(2,1)S(1)}, u32[]{:S(2)}, u32[]{:S(2)}) collective-permute-start(bf16[128,128]{1,0:T(8,128)(2,1)S(1)} %multiply_convert_fusion), channel_id=1, source_target_pairs={{1,0},{2,1},{3,2},{4,3},{5,4},{6,5},{7,6},{8,7},{9,8},{10,9},{11,1... | collective-permute-start | bytes 98312 | tf_op jit(solution)/shard_map/ppermute | solution.py:24
  239.9 7.2 %collective-permute-start.3 = (bf16[128,128]{1,0:T(8,128)(2,1)S(1)}, bf16[128,128]{1,0:T(8,128)(2,1)S(1)}, u32[]{:S(2)}, u32[]{:S(2)}) collective-permute-start(bf16[128,128]{1,0:T(8,128)(2,1)S(1)} %multiply_convert_fusion), channel_id=1, source_target_pairs={{2,0},{3,1},{4,2},{5,3},{6,4},{7,5},{8,6},{9,7},{10,8},{11,9},{12,... | collective-permute-start | bytes 98312 | tf_op jit(solution)/shard_map/ppermute | solution.py:24
  241.2 6.7 %collective-permute-start.4 = (bf16[128,128]{1,0:T(8,128)(2,1)S(1)}, bf16[128,128]{1,0:T(8,128)(2,1)S(1)}, u32[]{:S(2)}, u32[]{:S(2)}) collective-permute-start(bf16[128,128]{1,0:T(8,128)(2,1)S(1)} %multiply_convert_fusion), channel_id=1, source_target_pairs={{3,0},{4,1},{5,2},{6,3},{7,4},{8,5},{9,6},{10,7},{11,8},{12,9},{13... | collective-permute-start | bytes 98312 | tf_op jit(solution)/shard_map/ppermute | solution.py:24
  242.5 6.7 %collective-permute-start.5 = (bf16[128,128]{1,0:T(8,128)(2,1)S(1)}, bf16[128,128]{1,0:T(8,128)(2,1)S(1)}, u32[]{:S(2)}, u32[]{:S(2)}) collective-permute-start(bf16[128,128]{1,0:T(8,128)(2,1)S(1)} %multiply_convert_fusion), channel_id=1, source_target_pairs={{4,0},{5,1},{6,2},{7,3},{8,4},{9,5},{10,6},{11,7},{12,8},{13,9},{1... | collective-permute-start | bytes 98312 | tf_op jit(solution)/shard_map/ppermute | solution.py:24
  250.1 55.1 %copy-start.2 = (s32[4]{0:T(128)S(1)}, s32[4]{0:T(128)}, u32[]{:S(2)}) copy-start(s32[4]{0:T(128)} %param.17) | copy-start | bytes 52
Sparse Core Ops, SparseCore 0:
  250.3 52.4 all-gather.2
